TPU v7x, 1024 devices: a whole 8x8x8 slice. The times are simulated.
1024 devices in a mesh: dom: 128 (over x, y, core), band: 8 (over z).
Axes of the slice: x: 8, y: 8, z: 8, core: 2. Of those that a mesh axis runs over, the one named last changes fastest.
Arguments:
- orbitals: float32 [16, 128, 4096], P('band', 'dom'), may hold values from -18 to 18
- potential: float32 [128, 4096], P('dom'), may hold values from -2 to 0
- support: int32 [65536], P('dom'), may hold values from 0 to 4095, as said below
- proj: float32 [16, 65536], P(None, 'dom'), may hold values from -0.125 to 0.125
- offsets: int32 [128], replicated, may hold values from 0 to 1023, as said below
- coupling: float32 [1024], replicated, may hold values from 0.2 to 1
Outputs:
- rotated: float32 [16, 128, 4096], P('band', 'dom')
- projected: float32 [16, 16], replicated
Inputs may be any that keep to these rules, and one draw needn't show every extreme that they name: `support`: on each domain the 512 entries are strictly increasing local cell indices; the first is 0 and the last is 4095. offsets[d] lies in [8 d, 8 (d + 1)).
All inputs are finite; a program needn't handle non-finite values.
Results may differ from a plain program's by a relative error of at most 0.0003.
Values sent between devices are 32-bit elements; how exact they have to be, the bound alone decides.
A program may use at most 32 MiB of HBM per device.

v0:
```python
import jax
import jax.numpy as jnp
from jax import lax
from jax.sharding import PartitionSpec as P

BX = 8
BY = 16
BZ = 32
DEG = 4
NS_ITERS = 10


STENCIL = [
    -5369.0 / 1800.0,
    12.0 / 7.0,
    -15.0 / 56.0,
    10.0 / 189.0,
    -1.0 / 112.0,
    2.0 / 1925.0,
    -1.0 / 16632.0,
]
CENTER = 10.0
HALF_WIDTH = 6.0


def shifted(block, axis, distance):
    devices = range(lax.axis_size(axis))
    route = [((i - distance) % len(devices), i) for i in devices]
    return lax.ppermute(block, axis, route)


def inverse_root(correlation):
    order = correlation.shape[0]
    norm_scale = jnp.sqrt(jnp.sum(correlation * correlation))
    iterate = correlation / norm_scale
    inverse = jnp.eye(order, dtype=jnp.float32)
    identity = jnp.eye(order, dtype=jnp.float32)
    for sweep in range(NS_ITERS):
        middle = 1.5 * identity - 0.5 * jnp.dot(inverse, iterate, precision=lax.Precision.HIGHEST)
        iterate = jnp.dot(iterate, middle, precision=lax.Precision.HIGHEST)
        inverse = jnp.dot(middle, inverse, precision=lax.Precision.HIGHEST)
    return inverse / jnp.sqrt(norm_scale)


def fetch(slab, step_by):
    return shifted(slab, "dom", step_by)


def extend(grid_block, axis_id, stride, sub_count, position, dom_count):
    extent = grid_block.shape[axis_id]
    upper_rim = lax.slice_in_dim(grid_block, extent - 6, extent, axis=axis_id)
    lower_rim = lax.slice_in_dim(grid_block, 0, 6, axis=axis_id)
    lower_halo = fetch(upper_rim, stride)
    upper_halo = fetch(lower_rim, -stride)
    if stride * sub_count < dom_count:
        lower_wrap = fetch(upper_rim, -(sub_count - 1) * stride)
        upper_wrap = fetch(lower_rim, (sub_count - 1) * stride)
        lower_halo = jnp.where(position == 0, lower_wrap, lower_halo)
        upper_halo = jnp.where(position == sub_count - 1, upper_wrap, upper_halo)
    return jnp.concatenate([lower_halo, grid_block, upper_halo], axis=axis_id)


def combine_projections(inner_prod, onehot):
    spread = jnp.dot(inner_prod, onehot, precision=lax.Precision.HIGHEST)
    totals = lax.psum(spread, "dom")
    return jnp.dot(totals, onehot.T, precision=lax.Precision.HIGHEST)


def apply_ham(grid_block, potential_grid, support, proj, couple_local, onehot, places, dom_count):
    ext_x = extend(grid_block, 1, places[0][0], places[0][1], places[0][2], dom_count)
    ext_y = extend(grid_block, 2, places[1][0], places[1][1], places[1][2], dom_count)
    ext_z = extend(grid_block, 3, places[2][0], places[2][1], places[2][2], dom_count)
    size_x = grid_block.shape[1]
    size_y = grid_block.shape[2]
    size_z = grid_block.shape[3]
    laplace = 3.0 * STENCIL[0] * grid_block
    for reach in range(1, 7):
        beside_all = (
            ext_x[:, 6 + reach : 6 + reach + size_x] + ext_x[:, 6 - reach : 6 - reach + size_x]
        )
        beside_all = (
            beside_all
            + ext_y[:, :, 6 + reach : 6 + reach + size_y]
            + ext_y[:, :, 6 - reach : 6 - reach + size_y]
        )
        beside_all = (
            beside_all
            + ext_z[:, :, :, 6 + reach : 6 + reach + size_z]
            + ext_z[:, :, :, 6 - reach : 6 - reach + size_z]
        )
        laplace = laplace + STENCIL[reach] * beside_all
    flat_field = grid_block.reshape(grid_block.shape[0], -1)
    picked = flat_field[:, support]
    inner_prod = jnp.dot(picked, proj.T, precision=lax.Precision.HIGHEST)
    own_coeffs = combine_projections(inner_prod, onehot)
    spread_back = jnp.dot(own_coeffs * couple_local[None, :], proj, precision=lax.Precision.HIGHEST)
    nonlocal_part = jnp.zeros_like(flat_field).at[:, support].add(spread_back)
    return (
        -0.5 * laplace + potential_grid[None] * grid_block + nonlocal_part.reshape(grid_block.shape)
    )


def local(orbitals, potential, support, proj, offsets, coupling):
    dom_count = lax.axis_size("dom")
    side_z = min(4, max(2, dom_count // 16))
    side_y = min(4, max(2, dom_count // 16))
    side_x = dom_count // (side_y * side_z)
    own_index = lax.axis_index("dom")
    places = (
        (side_y * side_z, side_x, own_index // (side_y * side_z)),
        (side_z, side_y, own_index // side_z % side_y),
        (1, side_z, own_index % side_z),
    )
    total_proj = coupling.shape[0]
    block_width = proj.shape[0]
    local_ids = jnp.arange(block_width, dtype=jnp.int32)
    own_offset = jnp.take(offsets, own_index)
    own_ids = (own_offset + local_ids) % total_proj
    onehot = (jnp.arange(total_proj, dtype=jnp.int32)[None, :] == own_ids[:, None]).astype(
        jnp.float32
    )
    couple_local = jnp.dot(onehot, coupling, precision=lax.Precision.HIGHEST)
    orb_dev = orbitals.shape[0]
    start_block = orbitals.reshape(orb_dev, BX, BY, BZ)
    potential_grid = potential.reshape(BX, BY, BZ)

    def hamilton(grid_block):
        return apply_ham(
            grid_block, potential_grid, support, proj, couple_local, onehot, places, dom_count
        )

    previous = start_block
    current = (hamilton(start_block) - CENTER * start_block) / HALF_WIDTH
    for degree in range(1, DEG):
        following = 2.0 * (hamilton(current) - CENTER * current) / HALF_WIDTH - previous
        previous = current
        current = following
    hfield = hamilton(current)
    filtered_flat = current.reshape(orb_dev, -1)
    hfield_flat = hfield.reshape(orb_dev, -1)
    orb_all = orb_dev * lax.axis_size("band")
    column = lax.axis_index("band") * orb_dev
    gathered_flat = lax.all_gather(filtered_flat, "band", axis=0, tiled=True)
    correlation_cols = jnp.dot(gathered_flat, filtered_flat.T, precision=lax.Precision.HIGHEST)
    hmat_cols = jnp.dot(gathered_flat, hfield_flat.T, precision=lax.Precision.HIGHEST)
    empty = jnp.zeros((orb_all, orb_all), jnp.float32)
    correlation_part = lax.dynamic_update_slice(empty, correlation_cols, (jnp.int32(0), column))
    hmat_part = lax.dynamic_update_slice(empty, hmat_cols, (jnp.int32(0), column))
    correlation, hmat = lax.psum((correlation_part, hmat_part), ("dom", "band"))
    coeffs = inverse_root(correlation)
    projected = jnp.dot(
        jnp.dot(coeffs.T, hmat, precision=lax.Precision.HIGHEST),
        coeffs,
        precision=lax.Precision.HIGHEST,
    )
    own_cols = lax.dynamic_slice(coeffs, (jnp.int32(0), column), (orb_all, orb_dev))
    rotated_flat = jnp.dot(own_cols.T, gathered_flat, precision=lax.Precision.HIGHEST)
    rotated = rotated_flat.reshape(orbitals.shape)
    return (rotated, projected)


def solution(mesh):
    return jax.shard_map(
        local,
        mesh=mesh,
        in_specs=(P("band", "dom", None), P("dom", None), P("dom"), P(None, "dom"), P(), P()),
        out_specs=(P("band", "dom", None), P()),
        check_vma=False,
    )
```

profile of v0, /device:TPU:1, one launch (start us, length us, event | category | flops | bytes accessed | tf_op | source)
XLA Modules:
  0.0 1681.5 jit_solution(8799266808636778690)
XLA Ops:
  2.4 9.6 collective-permute-start.8
  12.0 2.8 collective-permute-start.9
  14.8 1.9 collective-permute-start.6
  16.8 9.2 collective-permute-start.7
  26.0 1.9 collective-permute-start.5
  33.1 255.1 %psum.49 = f32[2,1024]{1,0:T(2,128)S(1)} all-reduce(f32[2,1024]{1,0:T(2,128)S(1)} %fusion.373), channel_id=1, replica_groups=mesh['dom'=128,'band'=8] {'dom'}, use_global_device_ids=true, to_apply=%region_0.1 | all-reduce | flops 2048 | bytes 16384 | tf_op jit(solution)/shard_map/psum | solution.py:65
  290.3 2.8 scatter_custom_fusion
  297.9 5.5 collective-permute-start.2
  303.4 3.1 collective-permute-start.1
  306.6 3.4 collective-permute-start
  314.4 4.6 collective-permute-start.15
  319.1 4.7 collective-permute-start.14
  325.2 3.9 collective-permute-start.18
  332.9 252.2 %psum.50 = f32[2,1024]{1,0:T(2,128)S(1)} all-reduce(f32[2,1024]{1,0:T(2,128)S(1)} %fusion.372), channel_id=1, replica_groups=mesh['dom'=128,'band'=8] {'dom'}, use_global_device_ids=true, to_apply=%region_2.3 | all-reduce | flops 2048 | bytes 16384 | tf_op jit(solution)/shard_map/psum | solution.py:65
  585.6 2.8 scatter_custom_fusion.1
  589.3 1.9 collective-permute-start.16
  591.2 7.6 collective-permute-start.17
  598.9 7.5 collective-permute-start.13
  610.3 4.8 collective-permute-start.10
  619.9 4.0 collective-permute-start.25
  623.9 4.9 collective-permute-start.24
  629.7 7.1 collective-permute-start.28
  640.5 250.7 %psum.51 = f32[2,1024]{1,0:T(2,128)S(1)} all-reduce(f32[2,1024]{1,0:T(2,128)S(1)} %fusion.371), channel_id=1, replica_groups=mesh['dom'=128,'band'=8] {'dom'}, use_global_device_ids=true, to_apply=%region_4.5 | all-reduce | flops 2048 | bytes 16384 | tf_op jit(solution)/shard_map/psum | solution.py:65
  891.8 2.8 scatter_custom_fusion.2
  895.5 1.9 collective-permute-start.26
  897.4 5.9 collective-permute-start.27
  903.3 7.5 collective-permute-start.23
  914.8 4.6 collective-permute-start.20
  923.8 4.0 collective-permute-start.35
  927.8 4.9 collective-permute-start.34
  933.5 7.1 collective-permute-start.38
  944.4 250.7 %psum.52 = f32[2,1024]{1,0:T(2,128)S(1)} all-reduce(f32[2,1024]{1,0:T(2,128)S(1)} %fusion.370), channel_id=1, replica_groups=mesh['dom'=128,'band'=8] {'dom'}, use_global_device_ids=true, to_apply=%region_6.7 | all-reduce | flops 2048 | bytes 16384 | tf_op jit(solution)/shard_map/psum | solution.py:65
  1196.3 2.8 scatter_custom_fusion.3
  1201.9 5.9 collective-permute-start.37
  1207.8 7.5 collective-permute-start.33
  1219.2 4.8 collective-permute-start.30
  1228.7 4.0 collective-permute-start.45
  1232.7 5.0 collective-permute-start.44
  1238.5 7.1 collective-permute-start.48
  1245.6 1.9 collective-permute-start.49
  1247.5 24.0 %all-gather = f32[8,2,4096]{2,1,0:T(2,128)S(1)} all-gather(f32[1,2,4096]{2,1,0:T(2,128)S(1)} %reshape.190), channel_id=1, replica_groups=mesh['dom'=128,'band'=8] {'band'}, dimensions={0}, use_global_device_ids=true | all-gather | bytes 294912 | tf_op jit(solution)/shard_map/all_gather | solution.py:143
  1274.7 256.4 %psum.54 = f32[2,1024]{1,0:T(2,128)S(1)} all-reduce(f32[2,1024]{1,0:T(2,128)S(1)} %fusion.369), channel_id=1, replica_groups=mesh['dom'=128,'band'=8] {'dom'}, use_global_device_ids=true, to_apply=%region_10.11 | all-reduce | flops 2048 | bytes 16384 | tf_op jit(solution)/shard_map/psum | solution.py:65
  1532.3 2.8 scatter_custom_fusion.4
  1536.0 1.9 collective-permute-start.46
  1538.2 2.6 collective-permute-start.47
  1540.8 7.5 collective-permute-start.43
  1552.2 4.6 collective-permute-start.40
  1560.9 113.4 %all-reduce = (f32[16,16]{1,0:T(8,128)S(1)}, f32[16,16]{1,0:T(8,128)S(1)}) all-reduce(f32[16,16]{1,0:T(8,128)S(1)} %dynamic_update_slice.6, f32[16,16]{1,0:T(8,128)S(1)} %dynamic_update_slice.7), channel_id=1, replica_groups=mesh['dom'=128,'band'=8] {'dom','band'}, use_global_device_ids=true, to_apply=%region_8.9 | all-reduce | flops 512 | bytes 4096 | tf_op jit(solution)/shard_map/psum | solution.py:149
  (227 shorter events, 84.6 us)
Async XLA Ops:
  2.4 291.6 %collective-permute-start.8 = (f32[2,8,16,6]{3,2,1,0:T(8,128)}, f32[2,8,16,6]{3,2,1,0:T(8,128)S(1)}, u32[]{:S(2)}, u32[]{:S(2)}) collective-permute-start(f32[2,8,16,6]{3,2,1,0:T(8,128)} %get-tuple-element.56), channel_id=1, source_target_pairs={{24,0},{32,8},{40,16},{48,24},{56,32},{64,40},{72,48},{80,56},{88,... | collective-permute-start | bytes 18440 | tf_op jit(solution)/shard_map/ppermute | solution.py:29
  12.0 283.9 %collective-permute-start.9 = (f32[2,8,16,6]{3,2,1,0:T(8,128)}, f32[2,8,16,6]{3,2,1,0:T(8,128)S(1)}, u32[]{:S(2)}, u32[]{:S(2)}) collective-permute-start(f32[2,8,16,6]{3,2,1,0:T(8,128)} %get-tuple-element.56), channel_id=1, source_target_pairs={{1016,0},{0,8},{8,16},{16,24},{24,32},{32,40},{40,48},{48,56},{56,... | collective-permute-start | bytes 18440 | tf_op jit(solution)/shard_map/ppermute | solution.py:29
  14.8 283.1 %collective-permute-start.6 = (f32[2,8,16,6]{3,2,1,0:T(8,128)S(1)}, f32[2,8,16,6]{3,2,1,0:T(8,128)S(1)}, u32[]{:S(2)}, u32[]{:S(2)}) collective-permute-start(f32[2,8,16,6]{3,2,1,0:T(8,128)S(1)} %get-tuple-element.55), channel_id=1, source_target_pairs={{1000,0},{1008,8},{1016,16},{0,24},{8,32},{16,40},{24,48},{32,56},... | collective-permute-start | bytes 18440 | tf_op jit(solution)/shard_map/ppermute | solution.py:29
  16.8 286.6 %collective-permute-start.7 = (f32[2,8,16,6]{3,2,1,0:T(8,128)S(1)}, f32[2,8,16,6]{3,2,1,0:T(8,128)S(1)}, u32[]{:S(2)}, u32[]{:S(2)}) collective-permute-start(f32[2,8,16,6]{3,2,1,0:T(8,128)S(1)} %get-tuple-element.55), channel_id=1, source_target_pairs={{8,0},{16,8},{24,16},{32,24},{40,32},{48,40},{56,48},{64,56},{72,6... | collective-permute-start | bytes 18440 | tf_op jit(solution)/shard_map/ppermute | solution.py:29
  26.0 280.5 %collective-permute-start.5 = (f32[2,8,6,32]{3,1,2,0:T(8,128)S(1)}, f32[2,8,6,32]{3,1,2,0:T(8,128)}, u32[]{:S(2)}, u32[]{:S(2)}) collective-permute-start(f32[2,8,6,32]{3,1,2,0:T(8,128)S(1)} %copy.169), channel_id=1, source_target_pairs={{992,0},{1000,8},{1008,16},{1016,24},{0,32},{8,40},{16,48},{24,56}... | collective-permute-start | bytes 36872 | tf_op jit(solution)/shard_map/ppermute | solution.py:29
  294.0 16.0 collective-permute-start.4
  296.0 14.9 collective-permute-start.3
  297.9 12.9 collective-permute-start.2
  303.4 7.4 collective-permute-start.1
  314.4 295.8 %collective-permute-start.15 = (f32[2,8,6,32]{3,1,2,0:T(8,128)}, f32[2,8,6,32]{3,1,2,0:T(8,128)}, u32[]{:S(2)}, u32[]{:S(2)}) collective-permute-start(f32[2,8,6,32]{3,1,2,0:T(8,128)} %copy.180), channel_id=1, source_target_pairs={{992,0},{1000,8},{1008,16},{1016,24},{0,32},{8,40},{16,48},{24,56}... | collective-permute-start | bytes 36872 | tf_op jit(solution)/shard_map/ppermute | solution.py:29
  319.1 296.0 %collective-permute-start.14 = (f32[2,8,6,32]{3,1,2,0:T(8,128)}, f32[2,8,6,32]{3,1,2,0:T(8,128)}, u32[]{:S(2)}, u32[]{:S(2)}) collective-permute-start(f32[2,8,6,32]{3,1,2,0:T(8,128)} %copy.180), channel_id=1, source_target_pairs={{96,0},{104,8},{112,16},{120,24},{128,32},{136,40},{144,48},{152,5... | collective-permute-start | bytes 36872 | tf_op jit(solution)/shard_map/ppermute | solution.py:29
  325.2 266.0 %collective-permute-start.18 = (f32[2,8,16,6]{3,2,1,0:T(8,128)}, f32[2,8,16,6]{3,2,1,0:T(8,128)S(1)}, u32[]{:S(2)}, u32[]{:S(2)}) collective-permute-start(f32[2,8,16,6]{3,2,1,0:T(8,128)} %get-tuple-element.44), channel_id=1, source_target_pairs={{24,0},{32,8},{40,16},{48,24},{56,32},{64,40},{72,48},{80,56},{88,... | collective-permute-start | bytes 18440 | tf_op jit(solution)/shard_map/ppermute | solution.py:29
  329.1 269.7 %collective-permute-start.19 = (f32[2,8,16,6]{3,2,1,0:T(8,128)}, f32[2,8,16,6]{3,2,1,0:T(8,128)S(1)}, u32[]{:S(2)}, u32[]{:S(2)}) collective-permute-start(f32[2,8,16,6]{3,2,1,0:T(8,128)} %get-tuple-element.44), channel_id=1, source_target_pairs={{1016,0},{0,8},{8,16},{16,24},{24,32},{32,40},{40,48},{48,56},{56,... | collective-permute-start | bytes 18440 | tf_op jit(solution)/shard_map/ppermute | solution.py:29
  589.3 17.1 %collective-permute-start.16 = (f32[2,8,16,6]{3,2,1,0:T(8,128)S(1)}, f32[2,8,16,6]{3,2,1,0:T(8,128)S(1)}, u32[]{:S(2)}, u32[]{:S(2)}) collective-permute-start(f32[2,8,16,6]{3,2,1,0:T(8,128)S(1)} %get-tuple-element.43), channel_id=1, source_target_pairs={{1000,0},{1008,8},{1016,16},{0,24},{8,32},{16,40},{24,48},{32,56},... | collective-permute-start | bytes 18440 | tf_op jit(solution)/shard_map/ppermute | solution.py:29
  591.2 17.1 %collective-permute-start.17 = (f32[2,8,16,6]{3,2,1,0:T(8,128)S(1)}, f32[2,8,16,6]{3,2,1,0:T(8,128)S(1)}, u32[]{:S(2)}, u32[]{:S(2)}) collective-permute-start(f32[2,8,16,6]{3,2,1,0:T(8,128)S(1)} %get-tuple-element.43), channel_id=1, source_target_pairs={{8,0},{16,8},{24,16},{32,24},{40,32},{48,40},{56,48},{64,56},{72,6... | collective-permute-start | bytes 18440 | tf_op jit(solution)/shard_map/ppermute | solution.py:29
  598.9 17.1 %collective-permute-start.13 = (f32[2,8,6,32]{3,1,2,0:T(8,128)S(1)}, f32[2,8,6,32]{3,1,2,0:T(8,128)S(1)}, u32[]{:S(2)}, u32[]{:S(2)}) collective-permute-start(f32[2,8,6,32]{3,1,2,0:T(8,128)S(1)} %copy.176), channel_id=1, source_target_pairs={{32,0},{40,8},{48,16},{56,24},{64,32},{72,40},{80,48},{88,56},{96,... | collective-permute-start | bytes 36872 | tf_op jit(solution)/shard_map/ppermute | solution.py:29
  606.4 9.5 collective-permute-start.12
  608.3 7.9 collective-permute-start.11
  610.3 7.3 collective-permute-start.10
  619.9 294.8 %collective-permute-start.25 = (f32[2,8,6,32]{3,1,2,0:T(8,128)}, f32[2,8,6,32]{3,1,2,0:T(8,128)S(1)}, u32[]{:S(2)}, u32[]{:S(2)}) collective-permute-start(f32[2,8,6,32]{3,1,2,0:T(8,128)} %copy.191), channel_id=1, source_target_pairs={{992,0},{1000,8},{1008,16},{1016,24},{0,32},{8,40},{16,48},{24,56}... | collective-permute-start | bytes 36872 | tf_op jit(solution)/shard_map/ppermute | solution.py:29
  623.9 295.4 %collective-permute-start.24 = (f32[2,8,6,32]{3,1,2,0:T(8,128)}, f32[2,8,6,32]{3,1,2,0:T(8,128)}, u32[]{:S(2)}, u32[]{:S(2)}) collective-permute-start(f32[2,8,6,32]{3,1,2,0:T(8,128)} %copy.191), channel_id=1, source_target_pairs={{96,0},{104,8},{112,16},{120,24},{128,32},{136,40},{144,48},{152,5... | collective-permute-start | bytes 36872 | tf_op jit(solution)/shard_map/ppermute | solution.py:29
  629.7 267.7 %collective-permute-start.28 = (f32[2,8,16,6]{3,2,1,0:T(8,128)S(1)}, f32[2,8,16,6]{3,2,1,0:T(8,128)S(1)}, u32[]{:S(2)}, u32[]{:S(2)}) collective-permute-start(f32[2,8,16,6]{3,2,1,0:T(8,128)S(1)} %get-tuple-element.38), channel_id=1, source_target_pairs={{24,0},{32,8},{40,16},{48,24},{56,32},{64,40},{72,48},{80,56},{88,... | collective-permute-start | bytes 18440 | tf_op jit(solution)/shard_map/ppermute | solution.py:29
  636.8 266.5 %collective-permute-start.29 = (f32[2,8,16,6]{3,2,1,0:T(8,128)S(1)}, f32[2,8,16,6]{3,2,1,0:T(8,128)S(1)}, u32[]{:S(2)}, u32[]{:S(2)}) collective-permute-start(f32[2,8,16,6]{3,2,1,0:T(8,128)S(1)} %get-tuple-element.38), channel_id=1, source_target_pairs={{1016,0},{0,8},{8,16},{16,24},{24,32},{32,40},{40,48},{48,56},{56,... | collective-permute-start | bytes 18440 | tf_op jit(solution)/shard_map/ppermute | solution.py:29
  895.5 15.4 collective-permute-start.26
  897.4 15.4 collective-permute-start.27
  903.3 16.9 %collective-permute-start.23 = (f32[2,8,6,32]{3,1,2,0:T(8,128)S(1)}, f32[2,8,6,32]{3,1,2,0:T(8,128)S(1)}, u32[]{:S(2)}, u32[]{:S(2)}) collective-permute-start(f32[2,8,6,32]{3,1,2,0:T(8,128)S(1)} %copy.187), channel_id=1, source_target_pairs={{32,0},{40,8},{48,16},{56,24},{64,32},{72,40},{80,48},{88,56},{96,... | collective-permute-start | bytes 36872 | tf_op jit(solution)/shard_map/ppermute | solution.py:29
  910.8 9.3 collective-permute-start.22
  912.8 7.9 collective-permute-start.21
  914.8 7.3 collective-permute-start.20
  923.8 295.4 %collective-permute-start.35 = (f32[2,8,6,32]{3,1,2,0:T(8,128)S(1)}, f32[2,8,6,32]{3,1,2,0:T(8,128)}, u32[]{:S(2)}, u32[]{:S(2)}) collective-permute-start(f32[2,8,6,32]{3,1,2,0:T(8,128)S(1)} %copy.202), channel_id=1, source_target_pairs={{992,0},{1000,8},{1008,16},{1016,24},{0,32},{8,40},{16,48},{24,56}... | collective-permute-start | bytes 36872 | tf_op jit(solution)/shard_map/ppermute | solution.py:29
  927.8 296.2 %collective-permute-start.34 = (f32[2,8,6,32]{3,1,2,0:T(8,128)S(1)}, f32[2,8,6,32]{3,1,2,0:T(8,128)}, u32[]{:S(2)}, u32[]{:S(2)}) collective-permute-start(f32[2,8,6,32]{3,1,2,0:T(8,128)S(1)} %copy.202), channel_id=1, source_target_pairs={{96,0},{104,8},{112,16},{120,24},{128,32},{136,40},{144,48},{152,5... | collective-permute-start | bytes 36872 | tf_op jit(solution)/shard_map/ppermute | solution.py:29
  933.5 268.4 %collective-permute-start.38 = (f32[2,8,16,6]{3,2,1,0:T(8,128)S(1)}, f32[2,8,16,6]{3,2,1,0:T(8,128)S(1)}, u32[]{:S(2)}, u32[]{:S(2)}) collective-permute-start(f32[2,8,16,6]{3,2,1,0:T(8,128)S(1)} %get-tuple-element.32), channel_id=1, source_target_pairs={{24,0},{32,8},{40,16},{48,24},{56,32},{64,40},{72,48},{80,56},{88,... | collective-permute-start | bytes 18440 | tf_op jit(solution)/shard_map/ppermute | solution.py:29
  940.6 267.2 %collective-permute-start.39 = (f32[2,8,16,6]{3,2,1,0:T(8,128)S(1)}, f32[2,8,16,6]{3,2,1,0:T(8,128)S(1)}, u32[]{:S(2)}, u32[]{:S(2)}) collective-permute-start(f32[2,8,16,6]{3,2,1,0:T(8,128)S(1)} %get-tuple-element.32), channel_id=1, source_target_pairs={{1016,0},{0,8},{8,16},{16,24},{24,32},{32,40},{40,48},{48,56},{56,... | collective-permute-start | bytes 18440 | tf_op jit(solution)/shard_map/ppermute | solution.py:29
  1199.9 15.4 collective-permute-start.36
  1201.9 15.4 collective-permute-start.37
  1207.8 17.1 %collective-permute-start.33 = (f32[2,8,6,32]{3,1,2,0:T(8,128)S(1)}, f32[2,8,6,32]{3,1,2,0:T(8,128)S(1)}, u32[]{:S(2)}, u32[]{:S(2)}) collective-permute-start(f32[2,8,6,32]{3,1,2,0:T(8,128)S(1)} %copy.198), channel_id=1, source_target_pairs={{32,0},{40,8},{48,16},{56,24},{64,32},{72,40},{80,48},{88,56},{96,... | collective-permute-start | bytes 36872 | tf_op jit(solution)/shard_map/ppermute | solution.py:29
  1215.3 9.6 collective-permute-start.32
  1217.3 7.9 collective-permute-start.31
  1228.7 323.5 %collective-permute-start.45 = (f32[2,8,6,32]{3,1,2,0:T(8,128)}, f32[2,8,6,32]{3,1,2,0:T(8,128)}, u32[]{:S(2)}, u32[]{:S(2)}) collective-permute-start(f32[2,8,6,32]{3,1,2,0:T(8,128)} %copy.215), channel_id=1, source_target_pairs={{992,0},{1000,8},{1008,16},{1016,24},{0,32},{8,40},{16,48},{24,56}... | collective-permute-start | bytes 36872 | tf_op jit(solution)/shard_map/ppermute | solution.py:29
  1232.7 324.1 %collective-permute-start.44 = (f32[2,8,6,32]{3,1,2,0:T(8,128)}, f32[2,8,6,32]{3,1,2,0:T(8,128)}, u32[]{:S(2)}, u32[]{:S(2)}) collective-permute-start(f32[2,8,6,32]{3,1,2,0:T(8,128)} %copy.215), channel_id=1, source_target_pairs={{96,0},{104,8},{112,16},{120,24},{128,32},{136,40},{144,48},{152,5... | collective-permute-start | bytes 36872 | tf_op jit(solution)/shard_map/ppermute | solution.py:29
  1238.5 299.6 %collective-permute-start.48 = (f32[2,8,16,6]{3,2,1,0:T(8,128)S(1)}, f32[2,8,16,6]{3,2,1,0:T(8,128)S(1)}, u32[]{:S(2)}, u32[]{:S(2)}) collective-permute-start(f32[2,8,16,6]{3,2,1,0:T(8,128)S(1)} %get-tuple-element.26), channel_id=1, source_target_pairs={{24,0},{32,8},{40,16},{48,24},{56,32},{64,40},{72,48},{80,56},{88,... | collective-permute-start | bytes 18440 | tf_op jit(solution)/shard_map/ppermute | solution.py:29
  1245.6 295.1 %collective-permute-start.49 = (f32[2,8,16,6]{3,2,1,0:T(8,128)S(1)}, f32[2,8,16,6]{3,2,1,0:T(8,128)S(1)}, u32[]{:S(2)}, u32[]{:S(2)}) collective-permute-start(f32[2,8,16,6]{3,2,1,0:T(8,128)S(1)} %get-tuple-element.26), channel_id=1, source_target_pairs={{1016,0},{0,8},{8,16},{16,24},{24,32},{32,40},{40,48},{48,56},{56,... | collective-permute-start | bytes 18440 | tf_op jit(solution)/shard_map/ppermute | solution.py:29
  1536.0 12.3 collective-permute-start.46
  1538.2 12.1 collective-permute-start.47
  1540.8 16.9 %collective-permute-start.43 = (f32[2,8,6,32]{3,1,2,0:T(8,128)S(1)}, f32[2,8,6,32]{3,1,2,0:T(8,128)S(1)}, u32[]{:S(2)}, u32[]{:S(2)}) collective-permute-start(f32[2,8,6,32]{3,1,2,0:T(8,128)S(1)} %copy.211), channel_id=1, source_target_pairs={{32,0},{40,8},{48,16},{56,24},{64,32},{72,40},{80,48},{88,56},{96,... | collective-permute-start | bytes 36872 | tf_op jit(solution)/shard_map/ppermute | solution.py:29
  1548.3 9.4 collective-permute-start.42
  1550.2 7.8 collective-permute-start.41
  1552.2 7.1 collective-permute-start.40
  (10 other events, 963.1 us)
where the time goes:
time: 1680 us
  blocking collectives  1400 us (83%)
  starting transfers between devices  204 us (12%)
  local copies, waits for them, and re-layouts  25.2 us (2%)
  other arithmetic  24.8 us (1%)
    psum x5, blocking collectives, combine_projections(): totals = lax.psum(spread, 'dom')  1270 us
    ppermute x50, starting transfers between devices, shifted(): return lax.ppermute(block, axis, route)  204 us
    psum x1, blocking collectives, local(): correlation, hmat = lax.psum((correlation_part, hmat_part), ('dom', 'band'))  113 us
  transfers between devices with their start and end apart: 50, of which 9 were waited for; matrix products, arithmetic and copies ran while one was open for 3% of the time, Pallas kernels for 0%

commit v1 on v0

v1 whole, which is shorter than its diff:
```python
import functools

import jax
import jax.numpy as jnp
from jax import lax
from jax.experimental import pallas as pl
from jax.experimental.pallas import tpu as pltpu
from jax.sharding import PartitionSpec as P

DEG = 4
ROUNDS = DEG + 1
NS_ITERS = 10
NPROJ = 1024
PBLK = 16
SUPP = 512
DOMS = 128
BANDS = 8

STENCIL = [
    -5369.0 / 1800.0,
    12.0 / 7.0,
    -15.0 / 56.0,
    10.0 / 189.0,
    -1.0 / 112.0,
    2.0 / 1925.0,
    -1.0 / 16632.0,
]
HALF = [-0.5 * c for c in STENCIL]
CENTER = 10.0
HALF_WIDTH = 6.0
F32 = jnp.float32
BF16 = jnp.bfloat16
NT = (((1,), (1,)), ((), ()))


def roll(v, shift, axis):
    return pltpu.roll(v, shift % v.shape[axis], axis)


def iota(shape, axis):
    return lax.broadcasted_iota(jnp.int32, shape, axis)


def split3(v):
    high = v.astype(BF16)
    rest = v - high.astype(F32)
    mid = rest.astype(BF16)
    low = (rest - mid.astype(F32)).astype(BF16)
    return high, mid, low


def dot32(a, b):
    return jnp.dot(a, b, precision=lax.Precision.HIGHEST, preferred_element_type=F32)


def lane_z(shape):
    return iota(shape, len(shape) - 1) % 32


def lane_y(shape):
    return iota(shape, len(shape) - 1) // 32


def row_y(shape):
    return iota(shape, len(shape) - 2) % 4


def pack_y(v):
    pairs = v.reshape(4, 2, 8, 128)
    even, odd = pairs[:, 0], pairs[:, 1]
    yhi = row_y(even.shape)
    swapped = roll(even, 4, 1)
    first = jnp.where(yhi < 2, swapped, roll(odd, 6, 1))
    last = jnp.where(yhi >= 2, swapped, roll(odd, 2, 1))
    return first, last


def unpack_y(first, last):
    below = jnp.stack([last, roll(last, 2, 1)], axis=1).reshape(8, 8, 128)
    above = jnp.stack([first, roll(first, 6, 1)], axis=1).reshape(8, 8, 128)
    return below, above


def pack_z(v):
    quads = v.reshape(2, 4, 8, 128)
    z = lane_z((2, 8, 128))
    first, last = quads[:, 0], roll(quads[:, 0], 104, 2)
    for i in range(1, 4):
        inside = (z >= 8 * i) & (z < 8 * i + 8)
        first = jnp.where(inside, roll(quads[:, i], 8 * i, 2), first)
        last = jnp.where(inside, roll(quads[:, i], 104 + 8 * i, 2), last)
    return first, last


def unpack_z(first, last):
    above = jnp.stack([roll(first, 32 - 8 * i, 2) for i in range(4)], axis=1)
    below = jnp.stack([roll(last, 120 - 8 * i, 2) for i in range(4)], axis=1)
    return below.reshape(8, 8, 128), above.reshape(8, 8, 128)


def sum_x(v, below, above):
    ext = jnp.concatenate([below, v, above], axis=0)
    total = HALF[1] * (ext[7:15] + ext[5:13])
    for k in range(2, 7):
        total = total + HALF[k] * (ext[6 + k : 14 + k] + ext[6 - k : 14 - k])
    return total


def sum_y(v, below, above):
    yhi = row_y(v.shape)
    up1 = roll(jnp.where(yhi < 1, above, v), 7, 1)
    up2 = roll(jnp.where(yhi < 2, above, v), 6, 1)
    dn1 = roll(jnp.where(yhi >= 3, below, v), 1, 1)
    dn2 = roll(jnp.where(yhi >= 2, below, v), 2, 1)
    p = lane_y((1, 8, 128))
    h = HALF

    def pick(edge, upper, lower):
        return jnp.where(p >= edge, jnp.float32(upper), jnp.float32(lower))

    one = (
        pick(1, h[1], h[3]) * v
        + pick(1, h[5], h[1]) * up1
        + pick(1, 0.0, h[5]) * up2
        + pick(1, h[3], 0.0) * dn1
    )
    two = (
        h[2] * v
        + pick(2, h[6], h[2]) * up1
        + pick(2, 0.0, h[6]) * up2
        + pick(2, h[2], h[6]) * dn1
        + pick(2, h[6], 0.0) * dn2
    )
    three = (
        pick(3, h[3], h[1]) * v
        + pick(3, 0.0, h[3]) * up1
        + pick(3, h[1], h[5]) * dn1
        + pick(3, h[5], 0.0) * dn2
    )
    return h[4] * (up1 + dn1) + roll(one, 96, 2) + roll(two, 64, 2) + roll(three, 32, 2)


def sum_z(v, below, above):
    z = lane_z(v.shape)
    total = None
    for k in range(1, 7):
        up = roll(jnp.where(z < k, above, v), 128 - k, 2)
        down = roll(jnp.where(z >= 32 - k, below, v), k, 2)
        term = HALF[k] * (up + down)
        total = term if total is None else total + term
    return total


def spread_projectors(support, proj):
    high_bits = support // 128
    low_bits = support % 128
    rows = (iota((32, SUPP), 0) == high_bits).astype(F32)
    lanes = (iota((128, SUPP), 0) == low_bits).astype(F32).astype(BF16)
    dense = None
    for part in split3(proj):
        left = (part.astype(F32)[:, None, :] * rows[None]).reshape(PBLK * 32, SUPP)
        term = lax.dot_general(left.astype(BF16), lanes, NT, preferred_element_type=F32)
        dense = term if dense is None else dense + term
    dense = dense.reshape(PBLK * 4, 8, 128)
    turned = roll(dense, 4, 1)
    upper = iota(dense.shape, 1) < 4
    even = jnp.where(upper, dense, turned)
    odd = jnp.where(upper, turned, dense)
    return jnp.stack([even, odd], axis=1).reshape(PBLK, 8, 8, 128)


def flatten16(c):
    rep = jnp.concatenate([c] * 8, axis=1)
    own = iota((16, 128), 1) // 16 == iota((16, 128), 0) % 8
    rep = jnp.where(own, rep, 0.0)
    return jnp.sum(rep.reshape(2, 8, 128), axis=1)


def unflatten16(s):
    wide = jnp.concatenate(
        [jnp.broadcast_to(s[0:1], (8, 128)), jnp.broadcast_to(s[1:2], (8, 128))], axis=0
    )
    own = iota((16, 128), 1) // 16 == iota((16, 128), 0) % 8
    wide = jnp.where(own, wide, 0.0)
    for step in (16, 32, 64):
        wide = wide + roll(wide, step, 1)
    return wide


def kernel(
    orb, pot, sup, proj, off, coup, rot_out, prj_out,
    ys, pdense, match, yfirst, ylast, zfirst, zlast,
    xbelow, xabove, ybelow, yabove, zbelow, zabove, inner, hf,
    fslice, hslice, gathered, cz, cx, cy, hz, hx, hy,
    halo_send, halo_recv, inner_send, inner_recv,
    fs_send, fs_recv, hs_send, hs_recv, g_send, g_recv,
    cz_send, cz_recv, cx_send, cx_recv, cy_send, cy_recv,
    hz_send, hz_recv, hx_send, hx_recv, hy_send, hy_recv,
):
    me = lax.axis_index("dom")
    band = lax.axis_index("band")
    ax, ay = me // 16, me % 16
    by, cz_pos = (me // 4) % 4, me % 4

    def dom_x(i):
        return ((ax + i) % 8) * 16 + ay

    def dom_y(i):
        return ax * 16 + (ay + i) % 16

    x_up, x_down = dom_x(1), dom_x(7)
    y_up = ax * 16 + ((by + 1) % 4) * 4 + cz_pos
    y_down = ax * 16 + ((by + 3) % 4) * 4 + cz_pos
    z_up = me - cz_pos + (cz_pos + 1) % 4
    z_down = me - cz_pos + (cz_pos + 3) % 4
    chain = [((me + step) % DOMS, 2 - step) for step in (-2 + DOMS, -1 + DOMS, 1, 2)]
    chain = [(dom, slot + DOMS if slot < 0 else slot) for dom, slot in chain]

    barrier = pltpu.get_barrier_semaphore()
    greeted = [(dom_x(i), band) for i in range(1, 8)]
    greeted += [(dom_y(i), band) for i in range(1, 16)]
    greeted += [(me, (band + i) % BANDS) for i in range(1, 8)]
    greeted += [(dom, band) for dom, _ in chain]
    for device in greeted:
        pl.semaphore_signal(barrier, inc=1, device_id=device, device_id_type=pl.DeviceIdType.MESH)

    started = []

    def send(src, dst, ssem, rsem, dom, to_band):
        copy = pltpu.make_async_remote_copy(
            src_ref=src, dst_ref=dst, send_sem=ssem, recv_sem=rsem,
            device_id=(dom, to_band), device_id_type=pl.DeviceIdType.MESH,
        )
        copy.start()
        started.append(copy)

    def await_copy(src, dst, ssem, rsem):
        pltpu.make_async_remote_copy(
            src_ref=src, dst_ref=dst, send_sem=ssem, recv_sem=rsem,
            device_id=(me, band), device_id_type=pl.DeviceIdType.MESH,
        ).wait_recv()

    def share(buf, ssem, rsem, pos, count, place):
        for i in range(1, count):
            dom, to_band = place(i)
            send(buf.at[pos], buf.at[pos], ssem.at[i], rsem.at[pos], dom, to_band)

    def await_shares(buf, ssem, rsem, pos, count):
        for i in range(1, count):
            source = (pos + count - i) % count
            await_copy(buf.at[source], buf.at[source], ssem.at[i], rsem.at[source])

    def place_z(i):
        return me, (band + i) % BANDS

    def place_x(i):
        return dom_x(i), band

    def place_y(i):
        return dom_y(i), band

    def send_halos(k, v):
        y_first, y_last = pack_y(v)
        z_first, z_last = pack_z(v)
        yfirst[k], ylast[k] = y_first, y_last
        zfirst[k], zlast[k] = z_first, z_last
        block = ys.at[k]
        hs, hr = halo_send.at[k], halo_recv.at[k]
        send(yfirst.at[k], yabove.at[k], hs.at[0], hr.at[0], y_down, band)
        send(ylast.at[k], ybelow.at[k], hs.at[1], hr.at[1], y_up, band)
        send(block.at[pl.ds(0, 6)], xabove.at[k], hs.at[2], hr.at[2], x_down, band)
        send(block.at[pl.ds(2, 6)], xbelow.at[k], hs.at[3], hr.at[3], x_up, band)
        send(zfirst.at[k], zabove.at[k], hs.at[4], hr.at[4], z_down, band)
        send(zlast.at[k], zbelow.at[k], hs.at[5], hr.at[5], z_up, band)

    def send_inner(k, v):
        sums = jnp.concatenate([jnp.sum(pdense[j] * v, axis=0) for j in range(PBLK)], axis=0)
        ones = jnp.ones((8, 384), BF16)
        parts = jnp.concatenate(split3(sums), axis=1)
        flat = lax.dot_general(ones, parts, NT, preferred_element_type=F32)
        inner[k, 2] = flat[0:1]
        for i, (dom, slot) in enumerate(chain):
            send(inner.at[k, 2], inner.at[k, slot], inner_send.at[k, i], inner_recv.at[k, slot], dom, band)

    def apply_h(k, v, own, couple):
        hs, hr = halo_send.at[k], halo_recv.at[k]
        await_copy(zabove.at[k], zabove.at[k], hs.at[4], hr.at[4])
        await_copy(zbelow.at[k], zbelow.at[k], hs.at[5], hr.at[5])
        field = own * v + sum_z(v, *unpack_z(zabove[k], zbelow[k]))
        await_copy(xabove.at[k], xabove.at[k], hs.at[2], hr.at[2])
        await_copy(xbelow.at[k], xbelow.at[k], hs.at[3], hr.at[3])
        field = field + sum_x(v, xbelow[k], xabove[k])
        await_copy(yabove.at[k], yabove.at[k], hs.at[0], hr.at[0])
        await_copy(ybelow.at[k], ybelow.at[k], hs.at[1], hr.at[1])
        field = field + sum_y(v, *unpack_y(yabove[k], ybelow[k]))
        for i, (_, slot) in enumerate(chain):
            slot = 4 - slot
            await_copy(inner.at[k, slot], inner.at[k, slot], inner_send.at[k, i], inner_recv.at[k, slot])
        rows = jnp.concatenate([inner[k, slot] for slot in range(5)], axis=1)
        mine = (iota((8, 640), 1) // 4) % 2 == iota((8, 640), 0) // 4
        rows = jnp.where(mine, jnp.broadcast_to(rows, (8, 640)), 0.0)
        parts = [part.astype(F32) for part in split3(rows)]
        stacked = jnp.concatenate(parts + [jnp.zeros((8, 640), F32)], axis=0).astype(BF16)
        totals = jnp.dot(stacked, match[...], preferred_element_type=F32)
        coefs = (totals[0:8] + totals[8:16] + totals[16:24]) * couple
        for j in range(PBLK):
            field = field + jnp.broadcast_to(coefs[:, j : j + 1], (8, 128))[None] * pdense[j]
        return field

    ys[0, :, 0:4, :] = orb[0]
    ys[0, :, 4:8, :] = orb[1]
    current = ys[0]
    pots = jnp.concatenate([pot[...], pot[...]], axis=1)
    own = pots + jnp.float32(3.0 * HALF[0])
    pl.semaphore_wait(barrier, len(greeted))
    send_halos(0, current)
    pdense[...] = spread_projectors(sup[...], proj[...])
    send_inner(0, current)
    first_id = off[me]
    couple = jnp.zeros((1, 128), F32)
    lane = iota((1, 128), 1)
    for j in range(PBLK):
        couple = jnp.where(lane == j, coup[(first_id + j) % NPROJ], couple)
    wanted = (first_id + iota((128, 128), 1)) % NPROJ
    for slot in range(5):
        theirs = off[(me + slot - 2 + DOMS) % DOMS]
        have = (theirs + iota((128, 128), 0) // 8) % NPROJ
        match[slot * 128 : slot * 128 + 128, :] = jnp.where(have == wanted, 1.0, 0.0).astype(BF16)

    previous = current
    current = (apply_h(0, current, own, couple) - CENTER * current) * (1.0 / HALF_WIDTH)
    for k in range(1, DEG):
        ys[k] = current
        send_halos(k, current)
        send_inner(k, current)
        following = (apply_h(k, current, own, couple) - CENTER * current) * (2.0 / HALF_WIDTH) - previous
        previous, current = current, following
    ys[DEG] = current

    def spread_layers(block, buf, ssem, rsem):
        for i in range(1, BANDS):
            to = (band + i) % BANDS
            send(block.at[to], buf.at[band], ssem.at[i], rsem.at[band], me, to)
        buf[band] = block[band]

    def layer_rows(buf):
        flat = buf.reshape(64, 128)
        return jnp.concatenate([flat[pl.ds(y, 16, stride=4), :] for y in range(4)], axis=1)

    def product(a, b):
        return lax.dot_general(a, b, NT, precision=lax.Precision.HIGHEST, preferred_element_type=F32)

    spread_layers(ys.at[DEG], fslice, fs_send, fs_recv)
    send_halos(DEG, current)
    send_inner(DEG, current)
    await_shares(fslice, fs_send, fs_recv, band, BANDS)
    layer = layer_rows(fslice)
    cz[band] = flatten16(product(layer, layer))
    share(cz, cz_send, cz_recv, band, BANDS, place_z)
    hfield = apply_h(DEG, current, own, couple)
    hf[...] = hfield
    spread_layers(hf, hslice, hs_send, hs_recv)
    await_shares(cz, cz_send, cz_recv, band, BANDS)
    cx[ax] = jnp.sum(cz[...], axis=0)
    share(cx, cx_send, cx_recv, ax, 8, place_x)
    await_shares(hslice, hs_send, hs_recv, band, BANDS)
    hz[band] = flatten16(product(layer, layer_rows(hslice)))
    share(hz, hz_send, hz_recv, band, BANDS, place_z)
    for i in range(1, BANDS):
        send(ys.at[DEG], gathered.at[band], g_send.at[i], g_recv.at[band], *place_z(i))
    gathered[band] = current
    await_shares(cx, cx_send, cx_recv, ax, 8)
    cy[ay] = jnp.sum(cx[...], axis=0)
    share(cy, cy_send, cy_recv, ay, 16, place_y)
    await_shares(hz, hz_send, hz_recv, band, BANDS)
    hx[ax] = jnp.sum(hz[...], axis=0)
    share(hx, hx_send, hx_recv, ax, 8, place_x)
    await_shares(cy, cy_send, cy_recv, ay, 16)
    corr = jnp.sum(cy[...], axis=0)
    norm2 = jnp.sum(jnp.sum(corr * corr, axis=1, keepdims=True), axis=0, keepdims=True)
    norm = jnp.sqrt(norm2)
    iterate = unflatten16(corr)[:, :16] / norm
    identity = jnp.where(iota((16, 16), 0) == iota((16, 16), 1), 1.0, 0.0).astype(F32)
    inverse = identity
    for sweep in range(NS_ITERS):
        middle = 1.5 * identity - 0.5 * dot32(inverse, iterate)
        iterate = dot32(iterate, middle)
        inverse = dot32(middle, inverse)
        if sweep == 2:
            await_shares(hx, hx_send, hx_recv, ax, 8)
            hy[ay] = jnp.sum(hx[...], axis=0)
            share(hy, hy_send, hy_recv, ay, 16, place_y)
    coeffs = inverse / jnp.sqrt(norm)

    wide = jnp.concatenate([coeffs] * 8, axis=1)
    columns = []
    for o in range(2):
        chosen = iota((16, 128), 1) == 2 * band + o
        column = jnp.sum(jnp.where(chosen, wide, 0.0), axis=1, keepdims=True)
        columns.append(jnp.broadcast_to(column, (16, 128)))
    await_shares(gathered, g_send, g_recv, band, BANDS)
    upper = iota((8, 128), 0) < 4

    def row(o, j):
        return jnp.broadcast_to(columns[o][j : j + 1], (8, 128))

    rotated = jnp.zeros((8, 8, 128), F32)
    for b in range(BANDS):
        block = gathered[b]
        straight = jnp.where(upper, row(0, 2 * b), row(1, 2 * b + 1))
        crossed = jnp.where(upper, row(0, 2 * b + 1), row(1, 2 * b))
        rotated = rotated + straight[None] * block + crossed[None] * roll(block, 4, 1)
    rot_out[0] = rotated[:, 0:4, :]
    rot_out[1] = rotated[:, 4:8, :]

    await_shares(hy, hy_send, hy_recv, ay, 16)
    hmat = unflatten16(jnp.sum(hy[...], axis=0))[:, :16]
    left = lax.dot_general(
        coeffs, hmat, (((0,), (0,)), ((), ())), precision=lax.Precision.HIGHEST, preferred_element_type=F32
    )
    prj_out[...] = dot32(left, coeffs)

    for copy in started:
        copy.wait_send()


def local(orbitals, potential, support, proj, offsets, coupling):
    dma = pltpu.SemaphoreType.DMA
    vmem = pl.BlockSpec(memory_space=pltpu.VMEM)
    smem = pl.BlockSpec(memory_space=pltpu.SMEM)
    block = (8, 8, 128)
    scratch = [
        pltpu.VMEM((ROUNDS,) + block, F32),
        pltpu.VMEM((PBLK,) + block, F32),
        pltpu.VMEM((640, 128), BF16),
        *[pltpu.VMEM((ROUNDS, 4, 8, 128), F32)] * 2,
        *[pltpu.VMEM((ROUNDS, 2, 8, 128), F32)] * 2,
        *[pltpu.VMEM((ROUNDS, 6, 8, 128), F32)] * 2,
        *[pltpu.VMEM((ROUNDS, 4, 8, 128), F32)] * 2,
        *[pltpu.VMEM((ROUNDS, 2, 8, 128), F32)] * 2,
        pltpu.VMEM((ROUNDS, 5, 1, 128), F32),
        pltpu.VMEM(block, F32),
        pltpu.VMEM(block, F32),
        pltpu.VMEM(block, F32),
        pltpu.VMEM((BANDS,) + block, F32),
        *[pltpu.VMEM((n, 2, 128), F32) for n in (8, 8, 16)] * 2,
        *[dma((ROUNDS, 6))] * 2,
        *[dma((ROUNDS, 5))] * 2,
        *[dma((BANDS,))] * 6,
        *[dma((n,)) for n in (8, 8, 8, 8, 16, 16)] * 2,
    ]
    rotated, projected = pl.pallas_call(
        kernel,
        out_shape=(
            jax.ShapeDtypeStruct((2, 8, 4, 128), F32),
            jax.ShapeDtypeStruct((16, 16), F32),
        ),
        in_specs=[vmem, vmem, vmem, vmem, smem, smem],
        out_specs=(vmem, vmem),
        scratch_shapes=scratch,
        compiler_params=pltpu.CompilerParams(
            collective_id=0, has_side_effects=True, vmem_limit_bytes=16 * 1024 * 1024
        ),
    )(
        orbitals.reshape(2, 8, 4, 128),
        potential.reshape(8, 4, 128),
        support.reshape(1, SUPP),
        proj,
        offsets,
        coupling,
    )
    return rotated.reshape(orbitals.shape), projected


def solution(mesh):
    return jax.shard_map(
        local,
        mesh=mesh,
        in_specs=(P("band", "dom", None), P("dom", None), P("dom"), P(None, "dom"), P(), P()),
        out_specs=(P("band", "dom", None), P()),
        check_vma=False,
    )
```

time: 1680 us -> 79.9 us (0.05)
  blocking collectives: 1400 us -> 0 us
  starting transfers between devices: 204 us -> 0 us
  Pallas kernels: 0 us -> 74.1 us
  other arithmetic: 24.8 us -> 0 us
  local copies, waits for them, and re-layouts: 25.2 us -> 4.8 us
    psum x6 -> x0, blocking collectives: 1380 us -> none  [the longest x5 1270 us: combine_projections(): totals = lax.psum(spread, 'dom')]
    ppermute x50 -> x0, starting transfers between devices: 204 us -> none  [shifted(): return lax.ppermute(block, axis, route)]
    pallas_call x0 -> x1, Pallas kernels: none -> 74.1 us  [local(): pl.pallas_call(kernel, out_shape=(jax.ShapeDtypeStruct((2, 8, 4, 128), F3...]
    all_gather x1 -> x0, blocking collectives: 24 us -> none  [local(): gathered_flat = lax.all_gather(filtered_flat, 'band', axis=0, tiled=True)]
  transfers between devices with their start and end apart: 50 -> 0, of which waited for: 9 -> 0; matrix products, arithmetic and copies ran while one was open for 3% -> 0% of each run, Pallas kernels for 0% -> 0%
where the time goes in v1:
time: 79.9 us; the launch traced here: 79.5 us
  Pallas kernels  74.1 us (93%)
  local copies, waits for them, and re-layouts  4.8 us (6%)
    pallas_call x1, Pallas kernels, local(): pl.pallas_call(kernel, out_shape=(jax.ShapeDtypeStruct((2, 8, 4, 128), F3...  74.1 us
    unnamed x14, local copies, waits for them, and re-layouts  4.8 us

profile of v1, /device:TPU:1, one launch (start us, length us, event | category | flops | bytes accessed | tf_op | source)
XLA Modules:
  0.0 79.5 jit_solution(3303107871161830145)
XLA Ops:
  0.6 0.0 copy-start.3
  0.6 0.0 copy-start.5
  0.7 0.7 copy-done.3
  1.3 0.0 copy-done.5
  1.3 0.0 copy-start
  1.3 0.8 copy-done
  2.1 0.0 copy-start.1
  2.1 0.8 copy-done.1
  2.8 0.0 copy-start.2
  2.8 0.7 copy-done.2
  3.6 0.0 copy-start.4
  3.6 0.7 copy-done.4
  4.2 74.1 %shard_map.77 = (f32[2,8,4,128]{3,2,1,0:T(4,128)S(1)}, f32[16,16]{1,0:T(8,128)S(1)}) custom-call(f32[2,8,4,128]{3,2,1,0:T(4,128)S(1)} %bitcast.5, f32[8,4,128]{2,1,0:T(4,128)S(1)} %bitcast.6, s32[1,512]{1,0:T(1,128)S(1)} %bitcast.7, f32[16,512]{1,0:T(8,128)S(1)} %copy-done.1, s32[128]{0:T(128)S(1)} %copy-done.5, f32[1024]{0:T(1024)S(1)} %copy-done.3), custom_call_target="tpu_custom_call" | custom-call | tf_op jit(solution)/shard_map/pallas_call | solution.py:452
  78.3 0.6 copy.11
  78.9 0.6 copy.12
Async XLA Ops:
  0.6 0.7 copy-start.3
  0.6 0.7 copy-start.5
  1.3 0.8 copy-start
  2.1 0.8 copy-start.1
  2.8 0.7 copy-start.2
  3.6 0.7 copy-start.4

commit v2 on v1

--- a/solution.py
+++ b/solution.py
@@ -49,8 +49,14 @@
     return high, mid, low
 
 
-def dot32(a, b):
-    return jnp.dot(a, b, precision=lax.Precision.HIGHEST, preferred_element_type=F32)
+def small_dot(a, b, order=range(16)):
+    terms = [
+        jnp.broadcast_to(a[:, col : col + 1], (16, 128)) * jnp.broadcast_to(b[r : r + 1, :], (16, 128))
+        for r, col in enumerate(order)
+    ]
+    while len(terms) > 1:
+        terms = [x + y for x, y in zip(terms[::2], terms[1::2])]
+    return terms[0]
 
 
 def lane_z(shape):
@@ -169,33 +175,33 @@
     return jnp.stack([even, odd], axis=1).reshape(PBLK, 8, 8, 128)
 
 
-def flatten16(c):
-    rep = jnp.concatenate([c] * 8, axis=1)
-    own = iota((16, 128), 1) // 16 == iota((16, 128), 0) % 8
-    rep = jnp.where(own, rep, 0.0)
-    return jnp.sum(rep.reshape(2, 8, 128), axis=1)
-
-
-def unflatten16(s):
-    wide = jnp.concatenate(
-        [jnp.broadcast_to(s[0:1], (8, 128)), jnp.broadcast_to(s[1:2], (8, 128))], axis=0
-    )
-    own = iota((16, 128), 1) // 16 == iota((16, 128), 0) % 8
-    wide = jnp.where(own, wide, 0.0)
-    for step in (16, 32, 64):
-        wide = wide + roll(wide, step, 1)
-    return wide
+def lane_sums(rows):
+    parts = jnp.concatenate(split3(rows), axis=1)
+    return lax.dot_general(jnp.ones((8, 384), BF16), parts, NT, preferred_element_type=F32)[0:1]
+
+
+def square(rows):
+    lane, line = iota((16, 128), 1), iota((16, 128), 0)
+    spread = jnp.concatenate([jnp.broadcast_to(rows[z : z + 1], (2, 128)) for z in range(BANDS)], axis=0)
+    spread = jnp.where((lane // 8) % 2 == line % 2, spread, 0.0)
+    source, target = iota((128, 128), 0), iota((128, 128), 1)
+    fold = jnp.where(target % 16 == 2 * (source // 16) + (source // 4) % 2, 1.0, 0.0).astype(BF16)
+    parts = jnp.concatenate(split3(spread), axis=0)
+    three = jnp.dot(parts, fold, preferred_element_type=F32)
+    half = three[0:16] + three[16:32] + three[32:48]
+    turned = jnp.concatenate([jnp.transpose(half)[0:16, 0:16]] * 8, axis=1)
+    return jnp.where((lane % 16) // 2 <= line // 2, half, turned)
 
 
 def kernel(
-    orb, pot, sup, proj, off, coup, rot_out, prj_out,
+    orb_hbm, pot_hbm, sup_hbm, proj_hbm, off_hbm, coup_hbm, rot_out, prj_out,
+    orb, pot, sup, proj, off, coup, load_sem,
     ys, pdense, match, yfirst, ylast, zfirst, zlast,
-    xbelow, xabove, ybelow, yabove, zbelow, zabove, inner, hf,
-    fslice, hslice, gathered, cz, cx, cy, hz, hx, hy,
-    halo_send, halo_recv, inner_send, inner_recv,
-    fs_send, fs_recv, hs_send, hs_recv, g_send, g_recv,
-    cz_send, cz_recv, cx_send, cx_recv, cy_send, cy_recv,
-    hz_send, hz_recv, hx_send, hx_recv, hy_send, hy_recv,
+    xbelow, xabove, ybelow, yabove, zbelow, zabove, inner,
+    earlier, later, cx, cy, cz, hx, hy, hz,
+    halo_send, halo_recv, inner_send, inner_recv, g_send, g_recv,
+    cx_send, cx_recv, cy_send, cy_recv, cz_send, cz_recv,
+    hx_send, hx_recv, hy_send, hy_recv, hz_send, hz_recv, later_in,
 ):
     me = lax.axis_index("dom")
     band = lax.axis_index("band")
@@ -217,12 +223,21 @@
     chain = [(dom, slot + DOMS if slot < 0 else slot) for dom, slot in chain]
 
     barrier = pltpu.get_barrier_semaphore()
-    greeted = [(dom_x(i), band) for i in range(1, 8)]
-    greeted += [(dom_y(i), band) for i in range(1, 16)]
-    greeted += [(me, (band + i) % BANDS) for i in range(1, 8)]
-    greeted += [(dom, band) for dom, _ in chain]
-    for device in greeted:
+    near = [(y_up, band), (y_down, band)] + [(dom, band) for dom, _ in chain]
+    near += [(x_up, band), (x_down, band), (z_up, band), (z_down, band)]
+    for device in near:
         pl.semaphore_signal(barrier, inc=1, device_id=device, device_id_type=pl.DeviceIdType.MESH)
+    for b in range(1, BANDS):
+        @pl.when(b > band)
+        def _(b=b):
+            pl.semaphore_signal(barrier, inc=1, device_id=(me, b), device_id_type=pl.DeviceIdType.MESH)
+
+    loads = []
+    for i, (src, dst) in enumerate(
+        [(orb_hbm, orb), (proj_hbm, proj), (sup_hbm, sup), (off_hbm, off), (pot_hbm, pot), (coup_hbm, coup)]
+    ):
+        loads.append(pltpu.make_async_copy(src, dst, load_sem.at[i]))
+        loads[-1].start()
 
     started = []
 
@@ -250,6 +265,12 @@
             source = (pos + count - i) % count
             await_copy(buf.at[source], buf.at[source], ssem.at[i], rsem.at[source])
 
+    def band_copy(b, buf):
+        return pltpu.make_async_remote_copy(
+            src_ref=ys.at[DEG], dst_ref=buf.at[band], send_sem=g_send.at[b], recv_sem=g_recv.at[band],
+            device_id=(me, b), device_id_type=pl.DeviceIdType.MESH,
+        )
+
     def place_z(i):
         return me, (band + i) % BANDS
 
@@ -259,28 +280,38 @@
     def place_y(i):
         return dom_y(i), band
 
-    def send_halos(k, v):
-        y_first, y_last = pack_y(v)
-        z_first, z_last = pack_z(v)
-        yfirst[k], ylast[k] = y_first, y_last
-        zfirst[k], zlast[k] = z_first, z_last
+    def pack(k, v):
+        yfirst[k], ylast[k] = pack_y(v)
+        zfirst[k], zlast[k] = pack_z(v)
+
+    def send_far(k):
         block = ys.at[k]
         hs, hr = halo_send.at[k], halo_recv.at[k]
         send(yfirst.at[k], yabove.at[k], hs.at[0], hr.at[0], y_down, band)
         send(ylast.at[k], ybelow.at[k], hs.at[1], hr.at[1], y_up, band)
         send(block.at[pl.ds(0, 6)], xabove.at[k], hs.at[2], hr.at[2], x_down, band)
         send(block.at[pl.ds(2, 6)], xbelow.at[k], hs.at[3], hr.at[3], x_up, band)
+
+    def send_near(k):
+        hs, hr = halo_send.at[k], halo_recv.at[k]
         send(zfirst.at[k], zabove.at[k], hs.at[4], hr.at[4], z_down, band)
         send(zlast.at[k], zbelow.at[k], hs.at[5], hr.at[5], z_up, band)
 
-    def send_inner(k, v):
-        sums = jnp.concatenate([jnp.sum(pdense[j] * v, axis=0) for j in range(PBLK)], axis=0)
-        ones = jnp.ones((8, 384), BF16)
-        parts = jnp.concatenate(split3(sums), axis=1)
-        flat = lax.dot_general(ones, parts, NT, preferred_element_type=F32)
-        inner[k, 2] = flat[0:1]
+    def project(k, v):
+        inner[k, 2] = lane_sums(
+            jnp.concatenate([jnp.sum(pdense[j] * v, axis=0) for j in range(PBLK)], axis=0)
+        )
+
+    def send_inner(k):
         for i, (dom, slot) in enumerate(chain):
             send(inner.at[k, 2], inner.at[k, slot], inner_send.at[k, i], inner_recv.at[k, slot], dom, band)
+
+    def exchange(k, v):
+        pack(k, v)
+        send_far(k)
+        project(k, v)
+        send_inner(k)
+        send_near(k)
 
     def apply_h(k, v, own, couple):
         hs, hr = halo_send.at[k], halo_recv.at[k]
@@ -307,15 +338,34 @@
             field = field + jnp.broadcast_to(coefs[:, j : j + 1], (8, 128))[None] * pdense[j]
         return field
 
+    for load in loads:
+        load.wait()
     ys[0, :, 0:4, :] = orb[0]
     ys[0, :, 4:8, :] = orb[1]
     current = ys[0]
+    pack(0, current)
+    pdense[...] = spread_projectors(sup[...], proj[...])
+    project(0, current)
+    for b in range(BANDS):
+        @pl.when(b > band)
+        def _(b=b):
+            earlier[b] = jnp.zeros((8, 8, 128), F32)
+
+        @pl.when(b <= band)
+        def _(b=b):
+            later[b] = jnp.zeros((8, 8, 128), F32)
+
+    pl.semaphore_wait(barrier, len(near) + band)
+    send_far(0)
+    send_inner(0)
+    send_near(0)
+    for b in range(BANDS - 1):
+        @pl.when(b < band)
+        def _(b=b):
+            pl.semaphore_signal(later_in, inc=1, device_id=(me, b), device_id_type=pl.DeviceIdType.MESH)
+
     pots = jnp.concatenate([pot[...], pot[...]], axis=1)
     own = pots + jnp.float32(3.0 * HALF[0])
-    pl.semaphore_wait(barrier, len(greeted))
-    send_halos(0, current)
-    pdense[...] = spread_projectors(sup[...], proj[...])
-    send_inner(0, current)
     first_id = off[me]
     couple = jnp.zeros((1, 128), F32)
     lane = iota((1, 128), 1)
@@ -331,94 +381,103 @@
     current = (apply_h(0, current, own, couple) - CENTER * current) * (1.0 / HALF_WIDTH)
     for k in range(1, DEG):
         ys[k] = current
-        send_halos(k, current)
-        send_inner(k, current)
+        exchange(k, current)
         following = (apply_h(k, current, own, couple) - CENTER * current) * (2.0 / HALF_WIDTH) - previous
         previous, current = current, following
     ys[DEG] = current
 
-    def spread_layers(block, buf, ssem, rsem):
-        for i in range(1, BANDS):
-            to = (band + i) % BANDS
-            send(block.at[to], buf.at[band], ssem.at[i], rsem.at[band], me, to)
-        buf[band] = block[band]
-
-    def layer_rows(buf):
-        flat = buf.reshape(64, 128)
-        return jnp.concatenate([flat[pl.ds(y, 16, stride=4), :] for y in range(4)], axis=1)
-
-    def product(a, b):
-        return lax.dot_general(a, b, NT, precision=lax.Precision.HIGHEST, preferred_element_type=F32)
-
-    spread_layers(ys.at[DEG], fslice, fs_send, fs_recv)
-    send_halos(DEG, current)
-    send_inner(DEG, current)
-    await_shares(fslice, fs_send, fs_recv, band, BANDS)
-    layer = layer_rows(fslice)
-    cz[band] = flatten16(product(layer, layer))
-    share(cz, cz_send, cz_recv, band, BANDS, place_z)
+    @pl.when(band < BANDS - 1)
+    def _():
+        pl.semaphore_wait(later_in, BANDS - 1 - band)
+
+    earlier[band] = current
+    exchange(DEG, current)
+    for b in reversed(range(BANDS)):
+        @pl.when(b > band)
+        def _(b=b):
+            band_copy(b, earlier).start()
+
+        @pl.when(b < band)
+        def _(b=b):
+            band_copy(b, later).start()
+
+    def columns_of(v):
+        upper = iota(v.shape, 1) < 4
+        other = roll(v, 4, 1)
+        both = [jnp.where(upper, v, other), jnp.where(upper, other, v)]
+        return lane_sums(
+            jnp.concatenate([jnp.sum(earlier[b] * both[o], axis=0) for b in range(BANDS) for o in range(2)], axis=0)
+        )
+
+    for b in range(BANDS - 1):
+        @pl.when(b < band)
+        def _(b=b):
+            await_copy(earlier.at[b], earlier.at[b], g_send.at[b], g_recv.at[b])
+
+    cx[ax] = columns_of(current)
+    share(cx, cx_send, cx_recv, ax, 8, place_x)
     hfield = apply_h(DEG, current, own, couple)
-    hf[...] = hfield
-    spread_layers(hf, hslice, hs_send, hs_recv)
-    await_shares(cz, cz_send, cz_recv, band, BANDS)
-    cx[ax] = jnp.sum(cz[...], axis=0)
-    share(cx, cx_send, cx_recv, ax, 8, place_x)
-    await_shares(hslice, hs_send, hs_recv, band, BANDS)
-    hz[band] = flatten16(product(layer, layer_rows(hslice)))
-    share(hz, hz_send, hz_recv, band, BANDS, place_z)
-    for i in range(1, BANDS):
-        send(ys.at[DEG], gathered.at[band], g_send.at[i], g_recv.at[band], *place_z(i))
-    gathered[band] = current
+    hx[ax] = columns_of(hfield)
+    share(hx, hx_send, hx_recv, ax, 8, place_x)
     await_shares(cx, cx_send, cx_recv, ax, 8)
     cy[ay] = jnp.sum(cx[...], axis=0)
     share(cy, cy_send, cy_recv, ay, 16, place_y)
-    await_shares(hz, hz_send, hz_recv, band, BANDS)
-    hx[ax] = jnp.sum(hz[...], axis=0)
-    share(hx, hx_send, hx_recv, ax, 8, place_x)
+    await_shares(hx, hx_send, hx_recv, ax, 8)
+    hy[ay] = jnp.sum(hx[...], axis=0)
+    share(hy, hy_send, hy_recv, ay, 16, place_y)
     await_shares(cy, cy_send, cy_recv, ay, 16)
-    corr = jnp.sum(cy[...], axis=0)
-    norm2 = jnp.sum(jnp.sum(corr * corr, axis=1, keepdims=True), axis=0, keepdims=True)
+    cz[band] = jnp.sum(cy[...], axis=0)
+    share(cz, cz_send, cz_recv, band, BANDS, place_z)
+    await_shares(hy, hy_send, hy_recv, ay, 16)
+    hz[band] = jnp.sum(hy[...], axis=0)
+    share(hz, hz_send, hz_recv, band, BANDS, place_z)
+    await_shares(cz, cz_send, cz_recv, band, BANDS)
+    corr = square(jnp.concatenate([cz[b] for b in range(BANDS)], axis=0))
+
+    norm2 = jnp.sum(jnp.sum(corr * corr, axis=1, keepdims=True), axis=0, keepdims=True) * 0.125
     norm = jnp.sqrt(norm2)
-    iterate = unflatten16(corr)[:, :16] / norm
-    identity = jnp.where(iota((16, 16), 0) == iota((16, 16), 1), 1.0, 0.0).astype(F32)
-    inverse = identity
-    for sweep in range(NS_ITERS):
-        middle = 1.5 * identity - 0.5 * dot32(inverse, iterate)
-        iterate = dot32(iterate, middle)
-        inverse = dot32(middle, inverse)
-        if sweep == 2:
-            await_shares(hx, hx_send, hx_recv, ax, 8)
-            hy[ay] = jnp.sum(hx[...], axis=0)
-            share(hy, hy_send, hy_recv, ay, 16, place_y)
+    identity = jnp.where(iota((16, 128), 0) == iota((16, 128), 1) % 16, 1.0, 0.0).astype(F32)
+
+    def sweep(_, pair):
+        iterate, inverse = pair
+        middle = 1.5 * identity - 0.5 * small_dot(inverse, iterate)
+        return small_dot(iterate, middle), small_dot(middle, inverse)
+
+    _, inverse = lax.fori_loop(0, NS_ITERS, sweep, (corr / norm, identity))
     coeffs = inverse / jnp.sqrt(norm)
 
-    wide = jnp.concatenate([coeffs] * 8, axis=1)
     columns = []
     for o in range(2):
         chosen = iota((16, 128), 1) == 2 * band + o
-        column = jnp.sum(jnp.where(chosen, wide, 0.0), axis=1, keepdims=True)
+        column = jnp.sum(jnp.where(chosen, coeffs, 0.0), axis=1, keepdims=True)
         columns.append(jnp.broadcast_to(column, (16, 128)))
-    await_shares(gathered, g_send, g_recv, band, BANDS)
     upper = iota((8, 128), 0) < 4
 
     def row(o, j):
         return jnp.broadcast_to(columns[o][j : j + 1], (8, 128))
 
+    for b in range(1, BANDS):
+        @pl.when(b > band)
+        def _(b=b):
+            await_copy(later.at[b], later.at[b], g_send.at[b], g_recv.at[b])
+
     rotated = jnp.zeros((8, 8, 128), F32)
     for b in range(BANDS):
-        block = gathered[b]
+        block = earlier[b] + later[b]
         straight = jnp.where(upper, row(0, 2 * b), row(1, 2 * b + 1))
         crossed = jnp.where(upper, row(0, 2 * b + 1), row(1, 2 * b))
         rotated = rotated + straight[None] * block + crossed[None] * roll(block, 4, 1)
     rot_out[0] = rotated[:, 0:4, :]
     rot_out[1] = rotated[:, 4:8, :]
 
-    await_shares(hy, hy_send, hy_recv, ay, 16)
-    hmat = unflatten16(jnp.sum(hy[...], axis=0))[:, :16]
-    left = lax.dot_general(
-        coeffs, hmat, (((0,), (0,)), ((), ())), precision=lax.Precision.HIGHEST, preferred_element_type=F32
-    )
-    prj_out[...] = dot32(left, coeffs)
+    await_shares(hz, hz_send, hz_recv, band, BANDS)
+    hmat = square(jnp.concatenate([hz[b] for b in range(BANDS)], axis=0))
+    prj_out[...] = small_dot(small_dot(coeffs, hmat), coeffs)[:, 0:16]
+
+    for b in range(BANDS):
+        @pl.when(b != band)
+        def _(b=b):
+            band_copy(b, earlier).wait_send()
 
     for copy in started:
         copy.wait_send()
@@ -427,9 +486,16 @@
 def local(orbitals, potential, support, proj, offsets, coupling):
     dma = pltpu.SemaphoreType.DMA
     vmem = pl.BlockSpec(memory_space=pltpu.VMEM)
-    smem = pl.BlockSpec(memory_space=pltpu.SMEM)
+    anywhere = pl.BlockSpec(memory_space=pl.ANY)
     block = (8, 8, 128)
     scratch = [
+        pltpu.VMEM((2, 8, 4, 128), F32),
+        pltpu.VMEM((8, 4, 128), F32),
+        pltpu.VMEM((1, SUPP), jnp.int32),
+        pltpu.VMEM((PBLK, SUPP), F32),
+        pltpu.SMEM((DOMS,), jnp.int32),
+        pltpu.SMEM((NPROJ,), F32),
+        dma((6,)),
         pltpu.VMEM((ROUNDS,) + block, F32),
         pltpu.VMEM((PBLK,) + block, F32),
         pltpu.VMEM((640, 128), BF16),
@@ -439,15 +505,13 @@
         *[pltpu.VMEM((ROUNDS, 4, 8, 128), F32)] * 2,
         *[pltpu.VMEM((ROUNDS, 2, 8, 128), F32)] * 2,
         pltpu.VMEM((ROUNDS, 5, 1, 128), F32),
-        pltpu.VMEM(block, F32),
-        pltpu.VMEM(block, F32),
-        pltpu.VMEM(block, F32),
-        pltpu.VMEM((BANDS,) + block, F32),
-        *[pltpu.VMEM((n, 2, 128), F32) for n in (8, 8, 16)] * 2,
+        *[pltpu.VMEM((BANDS,) + block, F32)] * 2,
+        *[pltpu.VMEM((n, 1, 128), F32) for n in (8, 16, 8)] * 2,
         *[dma((ROUNDS, 6))] * 2,
         *[dma((ROUNDS, 5))] * 2,
-        *[dma((BANDS,))] * 6,
-        *[dma((n,)) for n in (8, 8, 8, 8, 16, 16)] * 2,
+        *[dma((BANDS,))] * 2,
+        *[dma((n,)) for n in (8, 8, 16, 16, 8, 8)] * 2,
+        pltpu.SemaphoreType.REGULAR,
     ]
     rotated, projected = pl.pallas_call(
         kernel,
@@ -455,11 +519,11 @@
             jax.ShapeDtypeStruct((2, 8, 4, 128), F32),
             jax.ShapeDtypeStruct((16, 16), F32),
         ),
-        in_specs=[vmem, vmem, vmem, vmem, smem, smem],
+        in_specs=[anywhere] * 6,
         out_specs=(vmem, vmem),
         scratch_shapes=scratch,
         compiler_params=pltpu.CompilerParams(
-            collective_id=0, has_side_effects=True, vmem_limit_bytes=16 * 1024 * 1024
+            collective_id=0, has_side_effects=True, vmem_limit_bytes=60 * 1024 * 1024
         ),
     )(
         orbitals.reshape(2, 8, 4, 128),

time: 79.9 us -> 64.6 us (0.81)
  Pallas kernels: 74.1 us -> 61.7 us
  local copies, waits for them, and re-layouts: 4.8 us -> 1.98 us
    pallas_call x1, Pallas kernels: 74.1 us -> 61.7 us  [local(): pl.pallas_call(kernel, out_shape=(jax.ShapeDtypeStruct((2, 8, 4, 128), F3...]
    unnamed x14 -> x4, local copies, waits for them, and re-layouts: 4.8 us -> 1.98 us
where the time goes in v2:
time: 64.6 us; the launch traced here: 64.4 us
  Pallas kernels  61.7 us (96%)
  local copies, waits for them, and re-layouts  1.98 us (3%)
  between operations  0.65 us (1%)
    pallas_call x1, Pallas kernels, local(): pl.pallas_call(kernel, out_shape=(jax.ShapeDtypeStruct((2, 8, 4, 128), F3...  61.7 us
    unnamed x4, local copies, waits for them, and re-layouts  1.98 us

profile of v2, /device:TPU:1, one launch (start us, length us, event | category | flops | bytes accessed | tf_op | source)
XLA Modules:
  0.0 64.4 jit_solution(17231972689308067989)
XLA Ops:
  0.6 61.7 %shard_map.77 = (f32[2,8,4,128]{3,2,1,0:T(4,128)}, f32[16,16]{1,0:T(8,128)}) custom-call(f32[2,8,4,128]{3,2,1,0:T(4,128)} %bitcast.5, f32[8,4,128]{2,1,0:T(4,128)} %bitcast.6, s32[1,512]{1,0:T(1,128)} %bitcast.7, f32[16,512]{1,0:T(8,128)} %proj_hbm.1, s32[128]{0:T(128)} %off_hbm.1, f32[1024]{0:T(1024)} %coup_hbm.1), custom_call_target="tpu_custom_call" | custom-call | tf_op jit(solution)/shard_map/pallas_call | solution.py:516
  62.4 0.0 copy-start
  62.4 1.4 %copy.11 = f32[2,1,4096]{2,1,0:T(1,128)} copy(f32[2,1,4096]{2,1,0:T(1,128)} %bitcast.4) | data formatting | bytes 65536
  63.8 0.0 copy-done
  63.8 0.6 copy.12
Async XLA Ops:
  62.4 1.4 %copy-start = (f32[16,16]{1,0:T(8,128)S(1)}, f32[16,16]{1,0:T(8,128)}, u32[]{:S(2)}) copy-start(f32[16,16]{1,0:T(8,128)} %get-tuple-element.11) | copy-start | bytes 3076

commit v3 on v2

--- a/solution.py
+++ b/solution.py
@@ -256,7 +256,7 @@
         ).wait_recv()
 
     def share(buf, ssem, rsem, pos, count, place):
-        for i in range(1, count):
+        for i in sorted(range(1, count), key=lambda i: abs(i - count // 2)):
             dom, to_band = place(i)
             send(buf.at[pos], buf.at[pos], ssem.at[i], rsem.at[pos], dom, to_band)
 
@@ -321,9 +321,6 @@
         await_copy(xabove.at[k], xabove.at[k], hs.at[2], hr.at[2])
         await_copy(xbelow.at[k], xbelow.at[k], hs.at[3], hr.at[3])
         field = field + sum_x(v, xbelow[k], xabove[k])
-        await_copy(yabove.at[k], yabove.at[k], hs.at[0], hr.at[0])
-        await_copy(ybelow.at[k], ybelow.at[k], hs.at[1], hr.at[1])
-        field = field + sum_y(v, *unpack_y(yabove[k], ybelow[k]))
         for i, (_, slot) in enumerate(chain):
             slot = 4 - slot
             await_copy(inner.at[k, slot], inner.at[k, slot], inner_send.at[k, i], inner_recv.at[k, slot])
@@ -336,6 +333,9 @@
         coefs = (totals[0:8] + totals[8:16] + totals[16:24]) * couple
         for j in range(PBLK):
             field = field + jnp.broadcast_to(coefs[:, j : j + 1], (8, 128))[None] * pdense[j]
+        await_copy(yabove.at[k], yabove.at[k], hs.at[0], hr.at[0])
+        await_copy(ybelow.at[k], ybelow.at[k], hs.at[1], hr.at[1])
+        field = field + sum_y(v, *unpack_y(yabove[k], ybelow[k]))
         return field
 
     for load in loads:
@@ -470,23 +470,25 @@
     rot_out[0] = rotated[:, 0:4, :]
     rot_out[1] = rotated[:, 4:8, :]
 
+    for copy in started[:-7]:
+        copy.wait_send()
+    for b in range(BANDS):
+        @pl.when(b != band)
+        def _(b=b):
+            band_copy(b, earlier).wait_send()
+
     await_shares(hz, hz_send, hz_recv, band, BANDS)
     hmat = square(jnp.concatenate([hz[b] for b in range(BANDS)], axis=0))
     prj_out[...] = small_dot(small_dot(coeffs, hmat), coeffs)[:, 0:16]
 
-    for b in range(BANDS):
-        @pl.when(b != band)
-        def _(b=b):
-            band_copy(b, earlier).wait_send()
-
-    for copy in started:
+    for copy in started[-7:]:
         copy.wait_send()
 
 
 def local(orbitals, potential, support, proj, offsets, coupling):
     dma = pltpu.SemaphoreType.DMA
     vmem = pl.BlockSpec(memory_space=pltpu.VMEM)
-    anywhere = pl.BlockSpec(memory_space=pl.ANY)
+    hbm = pl.BlockSpec(memory_space=pltpu.HBM)
     block = (8, 8, 128)
     scratch = [
         pltpu.VMEM((2, 8, 4, 128), F32),
@@ -519,19 +521,24 @@
             jax.ShapeDtypeStruct((2, 8, 4, 128), F32),
             jax.ShapeDtypeStruct((16, 16), F32),
         ),
-        in_specs=[anywhere] * 6,
+        in_specs=[hbm] * 6,
         out_specs=(vmem, vmem),
         scratch_shapes=scratch,
         compiler_params=pltpu.CompilerParams(
-            collective_id=0, has_side_effects=True, vmem_limit_bytes=60 * 1024 * 1024
+            collective_id=0, has_side_effects=True, vmem_limit_bytes=16 * 1024 * 1024
         ),
     )(
-        orbitals.reshape(2, 8, 4, 128),
-        potential.reshape(8, 4, 128),
-        support.reshape(1, SUPP),
-        proj,
-        offsets,
-        coupling,
+        *[
+            pltpu.with_memory_space_constraint(operand, pltpu.HBM)
+            for operand in (
+                orbitals.reshape(2, 8, 4, 128),
+                potential.reshape(8, 4, 128),
+                support.reshape(1, SUPP),
+                proj,
+                offsets,
+                coupling,
+            )
+        ]
     )
     return rotated.reshape(orbitals.shape), projected
 

time: 64.6 us -> 63.1 us (0.977)
  local copies, waits for them, and re-layouts: 1.98 us -> 1.22 us
  Pallas kernels: 61.7 us -> 61 us
    unnamed x4 -> x2, local copies, waits for them, and re-layouts: 1.98 us -> 1.22 us
    pallas_call x1, Pallas kernels: 61.7 us -> 61 us  [local(): pl.pallas_call(kernel, out_shape=(jax.ShapeDtypeStruct((2, 8, 4, 128), F3...]
where the time goes in v3:
time: 63.1 us; the launch traced here: 62.8 us
  Pallas kernels  61 us (97%)
  local copies, waits for them, and re-layouts  1.22 us (2%)
  between operations  0.64 us (1%)
    pallas_call x1, Pallas kernels, local(): pl.pallas_call(kernel, out_shape=(jax.ShapeDtypeStruct((2, 8, 4, 128), F3...  61 us

profile of v3, /device:TPU:1, one launch (start us, length us, event | category | flops | bytes accessed | tf_op | source)
XLA Modules:
  0.0 62.8 jit_solution(3638687583875262122)
XLA Ops:
  0.6 61.0 %shard_map.77 = (f32[2,8,4,128]{3,2,1,0:T(4,128)S(1)}, f32[16,16]{1,0:T(8,128)S(1)}) custom-call(f32[2,8,4,128]{3,2,1,0:T(4,128)} %bitcast.5, f32[8,4,128]{2,1,0:T(4,128)} %bitcast.6, s32[1,512]{1,0:T(1,128)} %bitcast.7, f32[16,512]{1,0:T(8,128)} %proj_hbm.1, s32[128]{0:T(128)} %off_hbm.1, f32[1024]{0:T(1024)} %coup_hbm.1), custom_call_target="tpu_custom_call" | custom-call | tf_op jit(solution)/shard_map/pallas_call | solution.py:518
  61.6 0.6 copy.11
  62.2 0.6 copy.12

commit v4 on v3

--- a/solution.py
+++ b/solution.py
@@ -307,10 +307,10 @@
             send(inner.at[k, 2], inner.at[k, slot], inner_send.at[k, i], inner_recv.at[k, slot], dom, band)
 
     def exchange(k, v):
+        project(k, v)
+        send_inner(k)
         pack(k, v)
         send_far(k)
-        project(k, v)
-        send_inner(k)
         send_near(k)
 
     def apply_h(k, v, own, couple):
@@ -397,10 +397,6 @@
         def _(b=b):
             band_copy(b, earlier).start()
 
-        @pl.when(b < band)
-        def _(b=b):
-            band_copy(b, later).start()
-
     def columns_of(v):
         upper = iota(v.shape, 1) < 4
         other = roll(v, 4, 1)
@@ -419,6 +415,11 @@
     hfield = apply_h(DEG, current, own, couple)
     hx[ax] = columns_of(hfield)
     share(hx, hx_send, hx_recv, ax, 8, place_x)
+    for b in range(BANDS - 1):
+        @pl.when(b < band)
+        def _(b=b):
+            band_copy(b, later).start()
+
     await_shares(cx, cx_send, cx_recv, ax, 8)
     cy[ay] = jnp.sum(cx[...], axis=0)
     share(cy, cy_send, cy_recv, ay, 16, place_y)

time: 63.1 us -> 61.6 us (0.976)
  Pallas kernels: 61 us -> 59.6 us
    pallas_call x1, Pallas kernels: 61 us -> 59.6 us  [local(): pl.pallas_call(kernel, out_shape=(jax.ShapeDtypeStruct((2, 8, 4, 128), F3...]
where the time goes in v4:
time: 61.6 us; the launch traced here: 61.4 us
  Pallas kernels  59.6 us (97%)
  local copies, waits for them, and re-layouts  1.22 us (2%)
  between operations  0.64 us (1%)
    pallas_call x1, Pallas kernels, local(): pl.pallas_call(kernel, out_shape=(jax.ShapeDtypeStruct((2, 8, 4, 128), F3...  59.6 us

profile of v4, /device:TPU:1, one launch (start us, length us, event | category | flops | bytes accessed | tf_op | source)
XLA Modules:
  0.0 61.4 jit_solution(17881546678127290428)
XLA Ops:
  0.6 59.6 %shard_map.77 = (f32[2,8,4,128]{3,2,1,0:T(4,128)S(1)}, f32[16,16]{1,0:T(8,128)S(1)}) custom-call(f32[2,8,4,128]{3,2,1,0:T(4,128)} %bitcast.5, f32[8,4,128]{2,1,0:T(4,128)} %bitcast.6, s32[1,512]{1,0:T(1,128)} %bitcast.7, f32[16,512]{1,0:T(8,128)} %proj_hbm.1, s32[128]{0:T(128)} %off_hbm.1, f32[1024]{0:T(1024)} %coup_hbm.1), custom_call_target="tpu_custom_call" | custom-call | tf_op jit(solution)/shard_map/pallas_call | solution.py:519
  60.2 0.6 %copy.11 = f32[2,1,4096]{2,1,0:T(1,128)} copy(f32[2,1,4096]{2,1,0:T(1,128)S(1)} %bitcast.4) | data formatting | bytes 65536
  60.8 0.6 copy.12

commit v5 on v4

--- a/solution.py
+++ b/solution.py
@@ -415,14 +415,14 @@
     hfield = apply_h(DEG, current, own, couple)
     hx[ax] = columns_of(hfield)
     share(hx, hx_send, hx_recv, ax, 8, place_x)
-    for b in range(BANDS - 1):
-        @pl.when(b < band)
-        def _(b=b):
-            band_copy(b, later).start()
-
     await_shares(cx, cx_send, cx_recv, ax, 8)
     cy[ay] = jnp.sum(cx[...], axis=0)
     share(cy, cy_send, cy_recv, ay, 16, place_y)
+    for b in range(BANDS - 1):
+        @pl.when(b < band)
+        def _(b=b):
+            band_copy(b, later).start()
+
     await_shares(hx, hx_send, hx_recv, ax, 8)
     hy[ay] = jnp.sum(hx[...], axis=0)
     share(hy, hy_send, hy_recv, ay, 16, place_y)

time: 61.6 us -> 61.7 us (level)
  no operation moved by 1% of the time
where the time goes in v5:
time: 61.7 us; the launch traced here: 61.5 us
  Pallas kernels  59.6 us (97%)
  local copies, waits for them, and re-layouts  1.22 us (2%)
  between operations  0.64 us (1%)
    pallas_call x1, Pallas kernels, local(): pl.pallas_call(kernel, out_shape=(jax.ShapeDtypeStruct((2, 8, 4, 128), F3...  59.6 us

profile of v5, /device:TPU:1, one launch (start us, length us, event | category | flops | bytes accessed | tf_op | source)
XLA Modules:
  0.0 61.5 jit_solution(13706254877205971100)
XLA Ops:
  0.6 59.6 %shard_map.77 = (f32[2,8,4,128]{3,2,1,0:T(4,128)S(1)}, f32[16,16]{1,0:T(8,128)S(1)}) custom-call(f32[2,8,4,128]{3,2,1,0:T(4,128)} %bitcast.5, f32[8,4,128]{2,1,0:T(4,128)} %bitcast.6, s32[1,512]{1,0:T(1,128)} %bitcast.7, f32[16,512]{1,0:T(8,128)} %proj_hbm.1, s32[128]{0:T(128)} %off_hbm.1, f32[1024]{0:T(1024)} %coup_hbm.1), custom_call_target="tpu_custom_call" | custom-call | tf_op jit(solution)/shard_map/pallas_call | solution.py:519
  60.3 0.6 %copy.11 = f32[2,1,4096]{2,1,0:T(1,128)} copy(f32[2,1,4096]{2,1,0:T(1,128)S(1)} %bitcast.4) | data formatting | bytes 65536
  60.9 0.6 copy.12
